TPU v7x, 32 devices: a whole 2x2x4 slice. The times are simulated.
32 devices in a mesh: groups: 2 (over x), pair: 16 (over z, y, core).
Axes of the slice: x: 2, y: 2, z: 4, core: 2. Of those that a mesh axis runs over, the one named last changes fastest.
Arguments:
- integrals: bfloat16 [6144, 2048], P('pair'), may hold values from -0.078125 to 0.078125
- probes: bfloat16 [12288, 128], P(('groups', 'pair')), parts along dimension 0, may hold values from -6 to 6
- occ_energy: float32 [8000], replicated, may hold values from -1.4 to -0.3
- vir_energy: float32 [32000], replicated, may hold values from 0.02 to 3
- block_occ: int32 [16], P('pair'), may hold values from 0 to 7999
- block_vir: int32 [16], P('pair'), may hold values from 0 to 249
- block_count: int32 [16], P('pair'), may hold values from 1 to 128, 1024 in all
- frequency: float32 [2], P('groups'), parts along dimension 0, may hold values from 0.1 to 2
Outputs:
- images: float32 [12288, 128], P(('groups', 'pair')), parts along dimension 0
There are 2 independent parts, one for each index of `groups`. A program takes and returns all parts, laid end to end along the dimension named above; an argument that names none is the same for every part. Nothing has to cross between parts.
Inputs may be any that keep to these rules, and one draw needn't show every extreme that they name: `block_count`: columns at and after a slot's count are padding; some slot has all 128 columns live.
All inputs are finite; a program needn't handle non-finite values. No bound on the sum of `block_count` on one device may be relied on, other than what follows from the above.
Results may differ from a plain program's by a relative error of at most 0.00051.
Values may be sent and summed in bfloat16 or wider, within the bound.
A program may use at most 64 MiB of HBM per device.

v0:
```python
import jax
import jax.numpy as jnp
from jax import lax
from jax.sharding import PartitionSpec as P


def contract_rows(left, right):
    return lax.dot_general(
        left, right, (((0,), (0,)), ((), ())), preferred_element_type=jnp.float32
    )


def on_device(
    integrals, probes, occ_energy, vir_energy, block_occ, block_vir, block_count, frequency
):
    column_index = jnp.arange(128, dtype=jnp.int32)
    live_cols = column_index[None, :] < block_count[:, None]
    vir_rows = vir_energy.reshape(-1, 128)[block_vir]
    energy_gap = vir_rows - occ_energy[block_occ][:, None]
    omega_val = frequency[0]
    ratio = 2.0 * energy_gap / (energy_gap * energy_gap + omega_val * omega_val)
    weights = jnp.where(live_cols, ratio, jnp.zeros_like(ratio)).reshape(-1)
    pair_major = lax.all_to_all(integrals, "pair", split_axis=1, concat_axis=0, tiled=True)
    projected = contract_rows(pair_major, lax.all_gather(probes, "pair", axis=0, tiled=True))
    weighted = (projected * weights[:, None]).astype(jnp.bfloat16)
    return jnp.dot(
        integrals,
        lax.all_gather(weighted, "pair", axis=0, tiled=True),
        preferred_element_type=jnp.float32,
    )


def solution(mesh):
    in_specs = (
        P("pair", None),
        P(("groups", "pair"), None),
        P(),
        P(),
        P("pair"),
        P("pair"),
        P("pair"),
        P("groups"),
    )
    out_specs = P(("groups", "pair"), None)
    return jax.shard_map(
        on_device, mesh=mesh, in_specs=in_specs, out_specs=out_specs, check_vma=False
    )
```

profile of v0, /device:TPU:0, one launch (start us, length us, event | category | flops | bytes accessed | tf_op | source)
XLA Modules:
  0.0 100.9 jit_solution(17537730710381882369)
XLA Ops:
  6.5 2.6 %copy.11 = bf16[384,2048]{0,1:T(8,128)(2,1)} copy(bf16[384,2048]{1,0:T(8,128)(2,1)} %param.8) | data formatting | bytes 3145728 | tf_op args[0]
  9.1 7.4 %all-to-all-start = ((bf16[384,16,128]{0,2,1:T(8,128)(2,1)}), bf16[384,16,128]{0,2,1:T(8,128)(2,1)S(1)}, u32[]{:S(2)}, u32[]{:S(2)}) async-start(bf16[384,16,128]{0,2,1:T(8,128)(2,1)} %bitcast), calls=%async_computation | async-start | bytes 3145728 | tf_op jit(solution)/shard_map/all_to_all | solution.py:23
  16.5 0.0 all-gather.2.cloned.1.call-start
  16.6 0.7 all-gather.2.cloned.1.call-update
  19.8 1.3 %dynamic-slice.6 = f32[1]{0:T(128)} dynamic-slice(f32[8000]{0:T(1024)} %param.10, s32[]{:T(128)} %bitcast.6), dynamic_slice_sizes={1} | dynamic-slice | bytes 12 | tf_op jit(solution)/shard_map/gather | solution.py:19
  21.1 1.3 %compare_select_fusion = f32[128]{0:T(128)S(1)} fusion(f32[250,128]{1,0:T(8,128)} %bitcast.20, s32[]{:T(128)} %bitcast.5, f32[]{:T(128)} %bitcast.8, f32[]{:T(128)} %bitcast.7, s32[]{:T(128)} %bitcast.17), kind=kLoop, calls=%fused_computation.3 | loop fusion | flops 896 | bytes 1040 | tf_op jit(solution)/shard_map/jit(_where)/select_n | solution.py:22
  22.4 29.3 %all-to-all-done = bf16[384,16,128]{0,2,1:T(8,128)(2,1)S(1)} async-done(((bf16[384,16,128]{0,2,1:T(8,128)(2,1)}), bf16[384,16,128]{0,2,1:T(8,128)(2,1)S(1)}, u32[]{:S(2)}, u32[]{:S(2)}) %all-to-all-start) | async-done | bytes 1572896 | tf_op jit(solution)/shard_map/all_to_all | solution.py:23
  51.6 0.9 copy.12
  52.6 17.3 %all-gather.2.cloned.1.call-done = bf16[6144,128]{1,0:T(8,128)(2,1)} async-done(((bf16[384,128]{1,0:T(8,128)(2,1)}), bf16[6144,128]{1,0:T(8,128)(2,1)}) %all-gather.2.cloned.1.call-update) | async-done | bytes 1572880 | tf_op jit(solution)/shard_map/all_gather | solution.py:24
  69.9 0.0 copy-start
  69.9 2.1 %fusion = bf16[128,128]{1,0:T(8,128)(2,1)S(1)} fusion(bf16[6144,128]{1,0:T(8,128)(2,1)S(1)} %bitcast.19, bf16[6144,128]{1,0:T(8,128)(2,1)} %all-gather.2.cloned.1.call-done, f32[128]{0:T(128)S(1)} %compare_select_fusion), kind=kOutput, calls=%fused_computation.2 | convolution fusion | flops 201359360 | bytes 3179008 | tf_op jit(solution)/shard_map/dot_general | solution.py:8
  72.1 20.5 %all_gather.7 = bf16[2048,128]{1,0:T(8,128)(2,1)S(1)} all-gather(bf16[128,128]{1,0:T(8,128)(2,1)S(1)} %fusion), channel_id=1, replica_groups=mesh['groups'=2,'pair'=16] {'pair'}, dimensions={0}, use_global_device_ids=true | all-gather | bytes 557056 | tf_op jit(solution)/shard_map/all_gather | solution.py:28
  92.6 0.0 copy-done
  92.6 0.6 convolution_bitcast_fusion
  93.2 0.8 copy.13
Async XLA Ops:
  9.1 42.5 %all-to-all-start = ((bf16[384,16,128]{0,2,1:T(8,128)(2,1)}), bf16[384,16,128]{0,2,1:T(8,128)(2,1)S(1)}, u32[]{:S(2)}, u32[]{:S(2)}) async-start(bf16[384,16,128]{0,2,1:T(8,128)(2,1)} %bitcast), calls=%async_computation | async-start | bytes 3145728 | tf_op jit(solution)/shard_map/all_to_all | solution.py:23
  16.5 53.4 %all-gather.2.cloned.1.call-start = ((), (), s32[]{:S(2)}) async-start(), calls=%async_computation.1 | async-start | bytes 1671168 | tf_op jit(solution)/shard_map/all_gather | solution.py:24
  69.9 22.7 %copy-start = (bf16[384,2048]{1,0:T(8,128)(2,1)S(1)}, bf16[384,2048]{1,0:T(8,128)(2,1)}, u32[]{:S(2)}) copy-start(bf16[384,2048]{1,0:T(8,128)(2,1)} %param.8) | copy-start | bytes 4718596
Sparse Core Ops, SparseCore 0:
  19.6 50.2 all-gather.1
where the time goes:
time: 101 us
  waiting for transfers between devices  47.3 us (47%)
  blocking collectives  20.5 us (20%)
  between operations  16 us (16%)
  starting transfers between devices  7.43 us (7%)
  local copies, waits for them, and re-layouts  5.62 us (6%)
  matrix products  2.74 us (3%)
  other arithmetic  1.26 us (1%)
    all_to_all x1, waiting for transfers between devices, on_device(): lax.all_to_all(integrals, 'pair', split_axis=1, concat_axis=0, tiled=True)  29.3 us
    all_gather x1, blocking collectives, on_device(): lax.all_gather(weighted, 'pair', axis=0, tiled=True)  20.5 us
    all_gather x1, waiting for transfers between devices, on_device(): lax.all_gather(probes, 'pair', axis=0, tiled=True)  17.3 us
    all_to_all x1, starting transfers between devices, on_device(): lax.all_to_all(integrals, 'pair', split_axis=1, concat_axis=0, tiled=True)  7.39 us
    unnamed x3, local copies, waits for them, and re-layouts  2.58 us
    dot_general x1, matrix products, contract_rows(): lax.dot_general(left, right, (((0,), (0,)), ((), ())), preferred_element_...  2.14 us
  transfers between devices with their start and end apart: 2, of which 2 were waited for; matrix products, arithmetic and copies ran while one was open for 3% of the time, Pallas kernels for 0%

commit v1 on v0

v1 whole, which is shorter than its diff:
```python
import functools

import jax
import jax.numpy as jnp
from jax import lax
from jax.experimental import pallas as pl
from jax.experimental.pallas import tpu as pltpu
from jax.sharding import PartitionSpec as P

LANES = 128


def kernel(
    nz, ny, integ_hbm, probes_hbm, vir_hbm, occ_ref, bocc_ref, bvir_ref, bcount_ref, freq_ref,
    out_ref,
    integ, probes, vir, partial, r1, r2, r3, gathered,
    in_sem, s1, v1, s2, v2, s3, v3, gzs, gzv, gys, gyv, gcs, gcv,
):
    nq = nz * ny
    me = lax.axis_index("pair")
    c = lax.rem(me, 2)
    q_me = me // 2
    y = lax.rem(q_me, ny)
    z = q_me // ny
    wide = 2 * LANES

    def dev(zz, yy, cc):
        return {"pair": (zz * ny + yy) * 2 + cc}

    mate = dev(z, y, 1 - c)
    ymate = dev(z, ny - 1 - y, c)

    def remote(src, dst, ss, rs, where):
        return pltpu.make_async_remote_copy(
            src_ref=src, dst_ref=dst, send_sem=ss, recv_sem=rs,
            device_id=where, device_id_type=pl.DeviceIdType.MESH,
        )

    loads = [pltpu.make_async_copy(probes_hbm, probes, in_sem.at[nq])]
    for q in range(nq):
        cols = pl.ds(q * wide, wide)
        loads.append(pltpu.make_async_copy(integ_hbm.at[:, cols], integ.at[:, cols], in_sem.at[q]))
    loads.append(pltpu.make_async_copy(vir_hbm, vir, in_sem.at[nq + 1]))
    for load in loads:
        load.start()

    barrier = pltpu.get_barrier_semaphore()
    peers = [mate] + ([ymate] if ny > 1 else [])
    peers += [dev(lax.rem(z + d, nz), y, c) for d in range(1, nz)]
    for peer in peers:
        pl.semaphore_signal(barrier, inc=1, device_id=peer, device_id_type=pl.DeviceIdType.MESH)

    sends = []
    loads[0].wait()
    for q in range(nq):
        loads[1 + q].wait()
        block = lax.dot_general(
            integ[:, q * wide:(q + 1) * wide], probes[...], (((0,), (0,)), ((), ())),
            preferred_element_type=jnp.float32,
        )
        partial[q] = block.reshape(2, LANES, LANES)
        if q == 0:
            pl.semaphore_wait(barrier, len(peers))
        copy = remote(partial.at[q, 1 - c], r1.at[q], s1.at[q], v1.at[q], mate)
        copy.start()
        sends.append(copy)
    core_copies = list(sends)

    loads[-1].wait()
    gap = vir[pl.ds(bvir_ref[0], 1), :] - occ_ref[bocc_ref[0]]
    omega = freq_ref[0]
    ratio = 2.0 * gap / (gap * gap + omega * omega)
    lane = lax.broadcasted_iota(jnp.int32, (1, LANES), 1)
    ratio = jnp.where(lane < bcount_ref[0], ratio, jnp.zeros_like(ratio))
    weights = jnp.transpose(jnp.broadcast_to(ratio, (LANES, LANES)))

    for q in range(nq):
        core_copies[q].wait_recv()

    order = [lax.rem(z + d, nz) for d in range(1, nz)] + [z]
    y_copies = []
    if ny > 1:
        for zz in order:
            qq = zz * ny + (ny - 1 - y)
            partial[qq, c] = partial[qq, c] + r1[qq]
            copy = remote(partial.at[qq, c], r2.at[zz], s2.at[zz], v2.at[zz], ymate)
            copy.start()
            y_copies.append(copy)
        sends += y_copies
    for d, zz in enumerate(order[:-1]):
        qq = zz * ny + y
        total = partial[qq, c] + r1[qq]
        if ny > 1:
            y_copies[d].wait_recv()
            total = total + r2[zz]
        partial[qq, c] = total
        copy = remote(partial.at[qq, c], r3.at[z], s3.at[zz], v3.at[z], dev(zz, y, c))
        copy.start()
        sends.append(copy)
    total = partial[q_me, c] + r1[q_me]
    if ny > 1:
        y_copies[-1].wait_recv()
        total = total + r2[z]
    for d in range(1, nz):
        zs = lax.rem(z + nz - d, nz)
        remote(r3.at[zs], r3.at[zs], s3.at[zs], v3.at[zs], dev(zs, y, c)).wait_recv()
        total = total + r3[zs]
    gathered[me] = (total * weights).astype(jnp.bfloat16)

    def spread(zs, yy):
        j = (zs * ny + yy) * 2 + c
        if True:
            copy = remote(gathered.at[j], gathered.at[j], gcs.at[j // 2], gcv.at[j // 2], mate)
            copy.start()
            sends.append(copy)

    def to_y(zs):
        j = (zs * ny + y) * 2 + c
        copy = remote(gathered.at[j], gathered.at[j], gys.at[zs], gyv.at[zs], ymate)
        copy.start()
        sends.append(copy)

    for d in range(1, nz):
        zz = lax.rem(z + d, nz)
        copy = remote(gathered.at[me], gathered.at[me], gzs.at[zz], gzv.at[z], dev(zz, y, c))
        copy.start()
        sends.append(copy)
    if ny > 1:
        to_y(z)
    spread(z, y)
    arrivals = [z]
    for d in range(1, nz):
        zs = lax.rem(z + nz - d, nz)
        arrivals.append(zs)
        j = (zs * ny + y) * 2 + c
        remote(gathered.at[j], gathered.at[j], gzs.at[zs], gzv.at[zs], dev(zs, y, c)).wait_recv()
        if ny > 1:
            to_y(zs)
        spread(zs, y)
    if ny > 1:
        for zs in arrivals:
            j = (zs * ny + (ny - 1 - y)) * 2 + c
            remote(gathered.at[j], gathered.at[j], gys.at[zs], gyv.at[zs], ymate).wait_recv()
            spread(zs, ny - 1 - y)

    group = ny * 2 * LANES
    for n, zs in enumerate(arrivals):
        for yy in range(ny):
            q = zs * ny + yy
            j = q * 2 + 1 - c
            remote(gathered.at[j], gathered.at[j], gcs.at[q], gcv.at[q], mate).wait_recv()
        rows = gathered[pl.ds(zs * ny * 2, ny * 2)].reshape(group, LANES)
        cols = pl.ds(pl.multiple_of(zs * group, group), group)
        term = jnp.dot(integ[:, cols], rows, preferred_element_type=jnp.float32)
        if n == 0:
            out_ref[...] = term
        else:
            out_ref[...] += term
    for copy in sends:
        copy.wait_send()


def solution(mesh):
    npair = mesh.shape["pair"]
    ny = 2 if npair == 16 else 1
    nz = npair // 2 // ny

    def on_device(integrals, probes, occ, vir, bocc, bvir, bcount, freq):
        aux, ncol = integrals.shape
        nq = nz * ny
        f32, bf16 = jnp.float32, jnp.bfloat16
        vir = vir.reshape(-1, LANES)
        dma = pltpu.SemaphoreType.DMA
        smem = pl.BlockSpec(memory_space=pltpu.SMEM)
        hbm = pl.BlockSpec(memory_space=pl.ANY)
        tile = (LANES, LANES)
        return pl.pallas_call(
            functools.partial(kernel, nz, ny),
            out_shape=jax.ShapeDtypeStruct((aux, LANES), f32),
            in_specs=[hbm, hbm, hbm] + [smem] * 5,
            out_specs=pl.BlockSpec(memory_space=pltpu.VMEM),
            scratch_shapes=[
                pltpu.VMEM((aux, ncol), bf16),
                pltpu.VMEM((aux, LANES), bf16),
                pltpu.VMEM(vir.shape, f32),
                pltpu.VMEM((nq, 2) + tile, f32),
                pltpu.VMEM((nq,) + tile, f32),
                pltpu.VMEM((nz,) + tile, f32),
                pltpu.VMEM((nz,) + tile, f32),
                pltpu.VMEM((npair,) + tile, bf16),
                dma((nq + 2,)),
                dma((nq,)), dma((nq,)),
                dma((nz,)), dma((nz,)),
                dma((nz,)), dma((nz,)),
                dma((nz,)), dma((nz,)),
                dma((nz,)), dma((nz,)),
                dma((nq,)), dma((nq,)),
            ],
            compiler_params=pltpu.CompilerParams(
                collective_id=0, has_side_effects=True, vmem_limit_bytes=40 * 1024 * 1024
            ),
            cost_estimate=pl.CostEstimate(
                flops=4 * aux * ncol * LANES, bytes_accessed=2 * aux * ncol, transcendentals=0
            ),
        )(integrals, probes, vir, occ, bocc, bvir, bcount, freq)

    in_specs = (
        P("pair", None), P(("groups", "pair"), None), P(), P(),
        P("pair"), P("pair"), P("pair"), P("groups"),
    )
    return jax.shard_map(
        on_device, mesh=mesh, in_specs=in_specs,
        out_specs=P(("groups", "pair"), None), check_vma=False,
    )
```

time: 101 us -> 37.8 us (0.37)
  waiting for transfers between devices: 47.3 us -> 0 us
  Pallas kernels: 0 us -> 30.3 us
  blocking collectives: 20.5 us -> 0 us
  between operations: 16 us -> 2.61 us
  starting transfers between devices: 7.43 us -> 0 us
  matrix products: 2.74 us -> 0 us
  other arithmetic: 1.26 us -> 0 us
    pallas_call x0 -> x1, Pallas kernels: none -> 30.3 us  [on_device(): pl.pallas_call(functools.partial(kernel, nz, ny), out_shape=jax.ShapeDtyp...]
    all_to_all x1 -> x0, waiting for transfers between devices: 29.3 us -> none  [on_device(): lax.all_to_all(integrals, 'pair', split_axis=1, concat_axis=0, tiled=True)]
    all_gather x1 -> x0, blocking collectives: 20.5 us -> none  [on_device(): lax.all_gather(weighted, 'pair', axis=0, tiled=True)]
    all_gather x1 -> x0, waiting for transfers between devices: 17.3 us -> none  [on_device(): lax.all_gather(probes, 'pair', axis=0, tiled=True)]
    all_to_all x1 -> x0, starting transfers between devices: 7.39 us -> none  [on_device(): lax.all_to_all(integrals, 'pair', split_axis=1, concat_axis=0, tiled=True)]
    dot_general x2 -> x0, matrix products: 2.74 us -> none  [the longest x1 2.14 us: contract_rows(): lax.dot_general(left, right, (((0,), (0,)), ((), ())), preferred_element_...]
    unnamed x3 -> x9, local copies, waits for them, and re-layouts: 2.58 us -> 4.63 us
    gather x1 -> x0, local copies, waits for them, and re-layouts: 1.27 us -> none  [on_device(): energy_gap = vir_rows - occ_energy[block_occ][:, None]]
  transfers between devices with their start and end apart: 2 -> 0, of which waited for: 2 -> 0; matrix products, arithmetic and copies ran while one was open for 3% -> 0% of each run, Pallas kernels for 0% -> 0%
where the time goes in v1:
time: 37.8 us; the launch traced here: 37.5 us
  Pallas kernels  30.3 us (80%)
  local copies, waits for them, and re-layouts  4.63 us (12%)
  between operations  2.61 us (7%)
    pallas_call x1, Pallas kernels, on_device(): pl.pallas_call(functools.partial(kernel, nz, ny), out_shape=jax.ShapeDtyp...  30.3 us
    unnamed x9, local copies, waits for them, and re-layouts  4.63 us

profile of v1, /device:TPU:0, one launch (start us, length us, event | category | flops | bytes accessed | tf_op | source)
XLA Modules:
  0.0 37.5 jit_solution(5312162102167454670)
XLA Ops:
  2.6 0.0 copy-start
  2.6 1.4 %copy-done = bf16[384,2048]{1,0:T(8,128)(2,1)S(1)} copy-done((bf16[384,2048]{1,0:T(8,128)(2,1)S(1)}, bf16[384,2048]{1,0:T(8,128)(2,1)}, u32[]{:S(2)}) %copy-start) | copy-done | bytes 1572888
  4.0 0.0 copy-start.1
  4.0 0.9 %copy-done.1 = f32[32000]{0:T(1024)S(1)} copy-done((f32[32000]{0:T(1024)S(1)}, f32[32000]{0:T(1024)}, u32[]{:S(2)}) %copy-start.1) | copy-done | bytes 128024
  4.9 0.0 copy-start.2
  4.9 0.9 %copy-done.2 = bf16[384,128]{1,0:T(8,128)(2,1)S(1)} copy-done((bf16[384,128]{1,0:T(8,128)(2,1)S(1)}, bf16[384,128]{1,0:T(8,128)(2,1)}, u32[]{:S(2)}) %copy-start.2) | copy-done | bytes 98328
  5.8 0.0 copy-start.3
  5.8 0.8 %copy-done.3 = f32[8000]{0:T(1024)S(1)} copy-done((f32[8000]{0:T(1024)S(1)}, f32[8000]{0:T(1024)}, u32[]{:S(2)}) %copy-start.3) | copy-done | bytes 32024
  6.6 30.3 %shard_map.82 = f32[384,128]{1,0:T(8,128)S(1)} custom-call(bf16[384,2048]{1,0:T(8,128)(2,1)S(1)} %copy-done, bf16[384,128]{1,0:T(8,128)(2,1)S(1)} %copy-done.2, f32[250,128]{1,0:T(8,128)S(1)} %bitcast.1, f32[8000]{0:T(1024)S(1)} %copy-done.3, s32[1]{0:T(128)S(6)} %copy.10.bocc_ref, s32[1]{0:T(128)S(6)} %copy.11.bvir_ref, s32[1]{0:T(128)S(6)} %copy.12.bcount_ref, ...), custom_call_target="tpu_custom_call" | custom-call | flops 402653184 | bytes 1572864 | tf_op jit(solution)/shard_map/pallas_call | solution.py:177
  36.8 0.7 %copy.14 = f32[384,128]{1,0:T(8,128)} copy(f32[384,128]{1,0:T(8,128)S(1)} %shard_map.82) | data formatting | bytes 393216
Async XLA Ops:
  2.6 1.4 %copy-start = (bf16[384,2048]{1,0:T(8,128)(2,1)S(1)}, bf16[384,2048]{1,0:T(8,128)(2,1)}, u32[]{:S(2)}) copy-start(bf16[384,2048]{1,0:T(8,128)(2,1)} %integ_hbm.1) | copy-start | bytes 4718596
  4.0 0.9 %copy-start.1 = (f32[32000]{0:T(1024)S(1)}, f32[32000]{0:T(1024)}, u32[]{:S(2)}) copy-start(f32[32000]{0:T(1024)} %param.11) | copy-start | bytes 384004
  4.9 0.9 %copy-start.2 = (bf16[384,128]{1,0:T(8,128)(2,1)S(1)}, bf16[384,128]{1,0:T(8,128)(2,1)}, u32[]{:S(2)}) copy-start(bf16[384,128]{1,0:T(8,128)(2,1)} %probes_hbm.1) | copy-start | bytes 294916
  5.8 0.8 %copy-start.3 = (f32[8000]{0:T(1024)S(1)}, f32[8000]{0:T(1024)}, u32[]{:S(2)}) copy-start(f32[8000]{0:T(1024)} %occ_ref.1) | copy-start | bytes 96004

commit v2 on v1

--- a/solution.py
+++ b/solution.py
@@ -11,9 +11,9 @@
 
 
 def kernel(
-    nz, ny, integ_hbm, probes_hbm, vir_hbm, occ_ref, bocc_ref, bvir_ref, bcount_ref, freq_ref,
+    nz, ny, integ_hbm, probes_hbm, vir_hbm, occ_hbm, bocc_hbm, bvir_hbm, bcount_hbm, freq_hbm,
     out_ref,
-    integ, probes, vir, partial, r1, r2, r3, gathered,
+    integ, probes, vir, occ, bocc_ref, bvir_ref, bcount_ref, freq_ref, partial, r1, r2, r3, gathered,
     in_sem, s1, v1, s2, v2, s3, v3, gzs, gzv, gys, gyv, gcs, gcv,
 ):
     nq = nz * ny
@@ -41,6 +41,12 @@
         cols = pl.ds(q * wide, wide)
         loads.append(pltpu.make_async_copy(integ_hbm.at[:, cols], integ.at[:, cols], in_sem.at[q]))
     loads.append(pltpu.make_async_copy(vir_hbm, vir, in_sem.at[nq + 1]))
+    small = (
+        (occ_hbm, occ), (bocc_hbm, bocc_ref), (bvir_hbm, bvir_ref),
+        (bcount_hbm, bcount_ref), (freq_hbm, freq_ref),
+    )
+    for n, (src, dst) in enumerate(small):
+        loads.append(pltpu.make_async_copy(src, dst, in_sem.at[nq + 2 + n]))
     for load in loads:
         load.start()
 
@@ -66,8 +72,9 @@
         sends.append(copy)
     core_copies = list(sends)
 
-    loads[-1].wait()
-    gap = vir[pl.ds(bvir_ref[0], 1), :] - occ_ref[bocc_ref[0]]
+    for load in loads[1 + nq:]:
+        load.wait()
+    gap = vir[pl.ds(bvir_ref[0], 1), :] - occ[bocc_ref[0]]
     omega = freq_ref[0]
     ratio = 2.0 * gap / (gap * gap + omega * omega)
     lane = lax.broadcasted_iota(jnp.int32, (1, LANES), 1)
@@ -109,10 +116,9 @@
 
     def spread(zs, yy):
         j = (zs * ny + yy) * 2 + c
-        if True:
-            copy = remote(gathered.at[j], gathered.at[j], gcs.at[j // 2], gcv.at[j // 2], mate)
-            copy.start()
-            sends.append(copy)
+        copy = remote(gathered.at[j], gathered.at[j], gcs.at[j // 2], gcv.at[j // 2], mate)
+        copy.start()
+        sends.append(copy)
 
     def to_y(zs):
         j = (zs * ny + y) * 2 + c
@@ -171,24 +177,26 @@
         f32, bf16 = jnp.float32, jnp.bfloat16
         vir = vir.reshape(-1, LANES)
         dma = pltpu.SemaphoreType.DMA
-        smem = pl.BlockSpec(memory_space=pltpu.SMEM)
-        hbm = pl.BlockSpec(memory_space=pl.ANY)
+        hbm = pl.BlockSpec(memory_space=pltpu.HBM)
         tile = (LANES, LANES)
         return pl.pallas_call(
             functools.partial(kernel, nz, ny),
             out_shape=jax.ShapeDtypeStruct((aux, LANES), f32),
-            in_specs=[hbm, hbm, hbm] + [smem] * 5,
+            in_specs=[hbm] * 8,
             out_specs=pl.BlockSpec(memory_space=pltpu.VMEM),
             scratch_shapes=[
                 pltpu.VMEM((aux, ncol), bf16),
                 pltpu.VMEM((aux, LANES), bf16),
                 pltpu.VMEM(vir.shape, f32),
+                pltpu.SMEM(occ.shape, f32),
+                pltpu.SMEM((1,), jnp.int32), pltpu.SMEM((1,), jnp.int32), pltpu.SMEM((1,), jnp.int32),
+                pltpu.SMEM((1,), f32),
                 pltpu.VMEM((nq, 2) + tile, f32),
                 pltpu.VMEM((nq,) + tile, f32),
                 pltpu.VMEM((nz,) + tile, f32),
                 pltpu.VMEM((nz,) + tile, f32),
                 pltpu.VMEM((npair,) + tile, bf16),
-                dma((nq + 2,)),
+                dma((nq + 7,)),
                 dma((nq,)), dma((nq,)),
                 dma((nz,)), dma((nz,)),
                 dma((nz,)), dma((nz,)),
@@ -197,7 +205,7 @@
                 dma((nq,)), dma((nq,)),
             ],
             compiler_params=pltpu.CompilerParams(
-                collective_id=0, has_side_effects=True, vmem_limit_bytes=40 * 1024 * 1024
+                collective_id=0, has_side_effects=True, vmem_limit_bytes=63 * 1024 * 1024
             ),
             cost_estimate=pl.CostEstimate(
                 flops=4 * aux * ncol * LANES, bytes_accessed=2 * aux * ncol, transcendentals=0

time: 37.8 us -> 33.7 us (0.89)
  local copies, waits for them, and re-layouts: 4.63 us -> 1.62 us
  Pallas kernels: 30.3 us -> 29.3 us
    unnamed x9 -> x1, local copies, waits for them, and re-layouts: 4.63 us -> 1.62 us
    pallas_call x1, Pallas kernels: 30.3 us -> 29.3 us  [on_device(): pl.pallas_call(functools.partial(kernel, nz, ny), out_shape=jax.ShapeDtyp...]
where the time goes in v2:
time: 33.7 us; the launch traced here: 33.5 us
  Pallas kernels  29.3 us (87%)
  between operations  2.59 us (8%)
  local copies, waits for them, and re-layouts  1.62 us (5%)
    pallas_call x1, Pallas kernels, on_device(): pl.pallas_call(functools.partial(kernel, nz, ny), out_shape=jax.ShapeDtyp...  29.3 us
    unnamed x1, local copies, waits for them, and re-layouts  1.62 us

profile of v2, /device:TPU:0, one launch (start us, length us, event | category | flops | bytes accessed | tf_op | source)
XLA Modules:
  0.0 33.5 jit_solution(17794322832166037659)
XLA Ops:
  2.6 29.3 %shard_map.82 = f32[384,128]{1,0:T(8,128)} custom-call(bf16[384,2048]{1,0:T(8,128)(2,1)} %integ_hbm.1, bf16[384,128]{1,0:T(8,128)(2,1)} %probes_hbm.1, f32[250,128]{1,0:T(8,128)} %bitcast.1, f32[8000]{0:T(1024)} %occ_hbm.1, s32[1]{0:T(128)S(6)} %copy.10.bocc_hbm, s32[1]{0:T(128)S(6)} %copy.11.bvir_hbm, s32[1]{0:T(128)S(6)} %copy.12.bcount_hbm, ...), custom_call_target="tpu_custom_call" | custom-call | flops 402653184 | bytes 1572864 | tf_op jit(solution)/shard_map/pallas_call | solution.py:182
  31.9 1.6 %copy.14 = f32[384,128]{1,0:T(8,128)} copy(f32[384,128]{1,0:T(8,128)} %shard_map.82) | data formatting | bytes 393216

commit v3 on v2

v3 whole, which is shorter than its diff:
```python
import functools

import jax
import jax.numpy as jnp
from jax import lax
from jax.experimental import pallas as pl
from jax.experimental.pallas import tpu as pltpu
from jax.sharding import PartitionSpec as P

LANES = 128
RS_PARTS = 2
AG_PARTS = 2


def kernel(
    nz, ny, integ_hbm, probes_hbm, vir_hbm, occ_hbm, bocc_hbm, bvir_hbm, bcount_hbm, freq_hbm,
    out_ref,
    integ, probes, vir, occ, bocc_ref, bvir_ref, bcount_ref, freq_ref, partial, r1, r2, r3, gathered,
    in_sem, s1, v1, s2, v2, s3, v3, gzs, gzv, gys, gyv, gcs, gcv,
):
    nq = nz * ny
    me = lax.axis_index("pair")
    c = lax.rem(me, 2)
    q_me = me // 2
    y = lax.rem(q_me, ny)
    z = q_me // ny
    wide = 2 * LANES

    def dev(zz, yy, cc):
        return {"pair": (zz * ny + yy) * 2 + cc}

    mate = dev(z, y, 1 - c)
    ymate = dev(z, ny - 1 - y, c)

    def remote(src, dst, ss, rs, where):
        return pltpu.make_async_remote_copy(
            src_ref=src, dst_ref=dst, send_sem=ss, recv_sem=rs,
            device_id=where, device_id_type=pl.DeviceIdType.MESH,
        )

    order = [lax.rem(z + d, nz) for d in range(1, nz)] + [z]
    blocks = [zz * ny + (ny - 1 - y) for zz in order] if ny > 1 else []
    blocks += [zz * ny + y for zz in order]

    def columns(q):
        return pl.ds(pl.multiple_of(q * wide, wide), wide)

    loads = [pltpu.make_async_copy(probes_hbm, probes, in_sem.at[nq])]
    for k, q in enumerate(blocks):
        loads.append(
            pltpu.make_async_copy(integ_hbm.at[:, columns(q)], integ.at[:, columns(q)], in_sem.at[k])
        )
    loads.append(pltpu.make_async_copy(vir_hbm, vir, in_sem.at[nq + 1]))
    small = (
        (occ_hbm, occ), (bocc_hbm, bocc_ref), (bvir_hbm, bvir_ref),
        (bcount_hbm, bcount_ref), (freq_hbm, freq_ref),
    )
    for n, (src, dst) in enumerate(small):
        loads.append(pltpu.make_async_copy(src, dst, in_sem.at[nq + 2 + n]))
    for load in loads:
        load.start()

    barrier = pltpu.get_barrier_semaphore()
    peers = [mate] + ([ymate] if ny > 1 else [])
    peers += [dev(lax.rem(z + d, nz), y, c) for d in range(1, nz)]
    for peer in peers:
        pl.semaphore_signal(barrier, inc=1, device_id=peer, device_id_type=pl.DeviceIdType.MESH)

    sends = []
    core_copies = []
    y_copies = []

    def to_mate(k, q):
        loads[1 + k].wait()
        block = lax.dot_general(
            integ[:, columns(q)], probes[...], (((0,), (0,)), ((), ())),
            preferred_element_type=jnp.float32,
        )
        partial[q] = block.reshape(2, RS_PARTS, LANES // RS_PARTS, LANES)
        if k == 0:
            pl.semaphore_wait(barrier, len(peers))
        copy = remote(partial.at[q, 1 - c], r1.at[q], s1.at[k], v1.at[k], mate)
        copy.start()
        sends.append(copy)
        core_copies.append(copy)

    def to_ymate(k):
        q, zz = blocks[k], order[k]
        core_copies[k].wait_recv()
        for h in range(RS_PARTS):
            partial[q, c, h] = partial[q, c, h] + r1[q, h]
            copy = remote(partial.at[q, c, h], r2.at[zz, h], s2.at[k, h], v2.at[k, h], ymate)
            copy.start()
            sends.append(copy)
            y_copies.append(copy)

    loads[0].wait()
    lag = 3
    n_y = nz if ny > 1 else 0
    for k, q in enumerate(blocks):
        to_mate(k, q)
        if 0 <= k - lag < n_y:
            to_ymate(k - lag)
    for k in range(max(0, nq - lag), n_y):
        to_ymate(k)

    for load in loads[1 + nq:]:
        load.wait()
    gap = vir[pl.ds(bvir_ref[0], 1), :] - occ[bocc_ref[0]]
    omega = freq_ref[0]
    ratio = 2.0 * gap / (gap * gap + omega * omega)
    lane = lax.broadcasted_iota(jnp.int32, (1, LANES), 1)
    ratio = jnp.where(lane < bcount_ref[0], ratio, jnp.zeros_like(ratio))
    weights = jnp.transpose(jnp.broadcast_to(ratio, (LANES, LANES)))

    for d, zz in enumerate(order[:-1]):
        q = blocks[n_y + d]
        core_copies[n_y + d].wait_recv()
        for h in range(RS_PARTS):
            total = partial[q, c, h] + r1[q, h]
            if ny > 1:
                y_copies[d * RS_PARTS + h].wait_recv()
                total = total + r2[zz, h]
            partial[q, c, h] = total
            copy = remote(partial.at[q, c, h], r3.at[z, h], s3.at[d, h], v3.at[z, h], dev(zz, y, c))
            copy.start()
            sends.append(copy)
    core_copies[-1].wait_recv()
    rows_r = LANES // RS_PARTS
    rows_a = LANES // AG_PARTS

    def to_z(h):
        for d in range(1, nz):
            zz = lax.rem(z + d, nz)
            copy = remote(
                gathered.at[me, h], gathered.at[me, h], gzs.at[zz, h], gzv.at[z, h], dev(zz, y, c)
            )
            copy.start()
            sends.append(copy)

    def to_y(zs, h):
        j = (zs * ny + y) * 2 + c
        copy = remote(gathered.at[j, h], gathered.at[j, h], gys.at[zs, h], gyv.at[zs, h], ymate)
        copy.start()
        sends.append(copy)

    def spread(zs, yy, h):
        j = (zs * ny + yy) * 2 + c
        q = zs * ny + yy
        copy = remote(gathered.at[j, h], gathered.at[j, h], gcs.at[q, h], gcv.at[q, h], mate)
        copy.start()
        sends.append(copy)

    done = 0
    for h in range(RS_PARTS):
        total = partial[q_me, c, h] + r1[q_me, h]
        if ny > 1:
            y_copies[(nz - 1) * RS_PARTS + h].wait_recv()
            total = total + r2[z, h]
        for d in range(1, nz):
            zs = lax.rem(z + nz - d, nz)
            remote(
                r3.at[zs, h], r3.at[zs, h], s3.at[d - 1, h], v3.at[zs, h], dev(zs, y, c)
            ).wait_recv()
            total = total + r3[zs, h]
        value = (total * weights[h * rows_r:(h + 1) * rows_r]).astype(jnp.bfloat16)
        if rows_a <= rows_r:
            per = rows_r // rows_a
            for g in range(per):
                gathered[me, h * per + g] = value[g * rows_a:(g + 1) * rows_a]
        else:
            per = rows_a // rows_r
            gathered[me, h // per, (h % per) * rows_r:(h % per + 1) * rows_r] = value
        while (done + 1) * rows_a <= (h + 1) * rows_r:
            to_z(done)
            if ny > 1:
                to_y(z, done)
            spread(z, y, done)
            done += 1
    arrivals = [z] + [lax.rem(z + nz - d, nz) for d in range(1, nz)]
    for h in range(AG_PARTS):
        for zs in arrivals[1:]:
            j = (zs * ny + y) * 2 + c
            remote(
                gathered.at[j, h], gathered.at[j, h], gzs.at[zs, h], gzv.at[zs, h], dev(zs, y, c)
            ).wait_recv()
            if ny > 1:
                to_y(zs, h)
            spread(zs, y, h)
    if ny > 1:
        for h in range(AG_PARTS):
            for zs in arrivals:
                j = (zs * ny + (ny - 1 - y)) * 2 + c
                remote(
                    gathered.at[j, h], gathered.at[j, h], gys.at[zs, h], gyv.at[zs, h], ymate
                ).wait_recv()
                spread(zs, ny - 1 - y, h)

    group = ny * 2 * LANES
    for n, zs in enumerate(arrivals):
        for yy in range(ny):
            q = zs * ny + yy
            j = q * 2 + 1 - c
            for h in range(AG_PARTS):
                remote(
                    gathered.at[j, h], gathered.at[j, h], gcs.at[q, h], gcv.at[q, h], mate
                ).wait_recv()
        rows = gathered[pl.ds(zs * ny * 2, ny * 2)].reshape(group, LANES)
        cols = pl.ds(pl.multiple_of(zs * group, group), group)
        term = jnp.dot(integ[:, cols], rows, preferred_element_type=jnp.float32)
        if n == 0:
            out_ref[...] = term
        else:
            out_ref[...] += term
    for copy in sends:
        copy.wait_send()


def solution(mesh):
    npair = mesh.shape["pair"]
    ny = 2 if npair == 16 else 1
    nz = npair // 2 // ny

    def on_device(integrals, probes, occ, vir, bocc, bvir, bcount, freq):
        aux, ncol = integrals.shape
        nq = nz * ny
        f32, bf16 = jnp.float32, jnp.bfloat16
        vir = vir.reshape(-1, LANES)
        dma = pltpu.SemaphoreType.DMA
        hbm = pl.BlockSpec(memory_space=pltpu.HBM)
        tile_r = (RS_PARTS, LANES // RS_PARTS, LANES)
        tile_a = (AG_PARTS, LANES // AG_PARTS, LANES)
        return pl.pallas_call(
            functools.partial(kernel, nz, ny),
            out_shape=jax.ShapeDtypeStruct((aux, LANES), f32),
            in_specs=[hbm] * 8,
            out_specs=pl.BlockSpec(memory_space=pltpu.VMEM),
            scratch_shapes=[
                pltpu.VMEM((aux, ncol), bf16),
                pltpu.VMEM((aux, LANES), bf16),
                pltpu.VMEM(vir.shape, f32),
                pltpu.SMEM(occ.shape, f32),
                pltpu.SMEM((1,), jnp.int32), pltpu.SMEM((1,), jnp.int32), pltpu.SMEM((1,), jnp.int32),
                pltpu.SMEM((1,), f32),
                pltpu.VMEM((nq, 2) + tile_r, f32),
                pltpu.VMEM((nq,) + tile_r, f32),
                pltpu.VMEM((nz,) + tile_r, f32),
                pltpu.VMEM((nz,) + tile_r, f32),
                pltpu.VMEM((npair,) + tile_a, bf16),
                dma((nq + 7,)),
                dma((nq,)), dma((nq,)),
                dma((nz, RS_PARTS)), dma((nz, RS_PARTS)),
                dma((nz, RS_PARTS)), dma((nz, RS_PARTS)),
                dma((nz, AG_PARTS)), dma((nz, AG_PARTS)),
                dma((nz, AG_PARTS)), dma((nz, AG_PARTS)),
                dma((nq, AG_PARTS)), dma((nq, AG_PARTS)),
            ],
            compiler_params=pltpu.CompilerParams(
                collective_id=0, has_side_effects=True, vmem_limit_bytes=63 * 1024 * 1024
            ),
            cost_estimate=pl.CostEstimate(
                flops=4 * aux * ncol * LANES, bytes_accessed=2 * aux * ncol, transcendentals=0
            ),
        )(integrals, probes, vir, occ, bocc, bvir, bcount, freq)

    in_specs = (
        P("pair", None), P(("groups", "pair"), None), P(), P(),
        P("pair"), P("pair"), P("pair"), P("groups"),
    )
    return jax.shard_map(
        on_device, mesh=mesh, in_specs=in_specs,
        out_specs=P(("groups", "pair"), None), check_vma=False,
    )
```

time: 33.7 us -> 31.2 us (0.926)
  Pallas kernels: 29.3 us -> 26.6 us
    pallas_call x1, Pallas kernels: 29.3 us -> 26.6 us  [on_device(): pl.pallas_call(functools.partial(kernel, nz, ny), out_shape=jax.ShapeDtyp...]
where the time goes in v3:
time: 31.2 us; the launch traced here: 30.9 us
  Pallas kernels  26.6 us (85%)
  between operations  2.59 us (8%)
  local copies, waits for them, and re-layouts  1.62 us (5%)
    pallas_call x1, Pallas kernels, on_device(): pl.pallas_call(functools.partial(kernel, nz, ny), out_shape=jax.ShapeDtyp...  26.6 us
    unnamed x1, local copies, waits for them, and re-layouts  1.62 us

profile of v3, /device:TPU:0, one launch (start us, length us, event | category | flops | bytes accessed | tf_op | source)
XLA Modules:
  0.0 30.9 jit_solution(8781456655884023449)
XLA Ops:
  2.6 26.6 %shard_map.82 = f32[384,128]{1,0:T(8,128)} custom-call(bf16[384,2048]{1,0:T(8,128)(2,1)} %integ_hbm.1, bf16[384,128]{1,0:T(8,128)(2,1)} %probes_hbm.1, f32[250,128]{1,0:T(8,128)} %bitcast.1, f32[8000]{0:T(1024)} %occ_hbm.1, s32[1]{0:T(128)S(6)} %copy.10.bocc_hbm, s32[1]{0:T(128)S(6)} %copy.11.bvir_hbm, s32[1]{0:T(128)S(6)} %copy.12.bcount_hbm, ...), custom_call_target="tpu_custom_call" | custom-call | flops 402653184 | bytes 1572864 | tf_op jit(solution)/shard_map/pallas_call | solution.py:233
  29.2 1.6 %copy.14 = f32[384,128]{1,0:T(8,128)} copy(f32[384,128]{1,0:T(8,128)} %shard_map.82) | data formatting | bytes 393216

commit v4 on v3

--- a/solution.py
+++ b/solution.py
@@ -19,6 +19,8 @@
     in_sem, s1, v1, s2, v2, s3, v3, gzs, gzv, gys, gyv, gcs, gcv,
 ):
     nq = nz * ny
+    rs_steps = sorted(range(1, nz), key=lambda d: abs(2 * d - nz))
+    ag_steps = sorted(range(1, nz), key=lambda d: abs(2 * d - nz))
     me = lax.axis_index("pair")
     c = lax.rem(me, 2)
     q_me = me // 2
@@ -38,7 +40,7 @@
             device_id=where, device_id_type=pl.DeviceIdType.MESH,
         )
 
-    order = [lax.rem(z + d, nz) for d in range(1, nz)] + [z]
+    order = [lax.rem(z + d, nz) for d in rs_steps] + [z]
     blocks = [zz * ny + (ny - 1 - y) for zz in order] if ny > 1 else []
     blocks += [zz * ny + y for zz in order]
 
@@ -95,7 +97,7 @@
             y_copies.append(copy)
 
     loads[0].wait()
-    lag = 3
+    lag = 2
     n_y = nz if ny > 1 else 0
     for k, q in enumerate(blocks):
         to_mate(k, q)
@@ -130,7 +132,7 @@
     rows_a = LANES // AG_PARTS
 
     def to_z(h):
-        for d in range(1, nz):
+        for d in ag_steps:
             zz = lax.rem(z + d, nz)
             copy = remote(
                 gathered.at[me, h], gathered.at[me, h], gzs.at[zz, h], gzv.at[z, h], dev(zz, y, c)
@@ -177,7 +179,7 @@
                 to_y(z, done)
             spread(z, y, done)
             done += 1
-    arrivals = [z] + [lax.rem(z + nz - d, nz) for d in range(1, nz)]
+    arrivals = [z] + [lax.rem(z + nz - d, nz) for d in ag_steps]
     for h in range(AG_PARTS):
         for zs in arrivals[1:]:
             j = (zs * ny + y) * 2 + c

time: 31.2 us -> 30.6 us (0.981)
  Pallas kernels: 26.6 us -> 26.1 us
    pallas_call x1, Pallas kernels: 26.6 us -> 26.1 us  [on_device(): pl.pallas_call(functools.partial(kernel, nz, ny), out_shape=jax.ShapeDtyp...]
where the time goes in v4:
time: 30.6 us; the launch traced here: 30.4 us
  Pallas kernels  26.1 us (85%)
  between operations  2.59 us (8%)
  local copies, waits for them, and re-layouts  1.62 us (5%)
    pallas_call x1, Pallas kernels, on_device(): pl.pallas_call(functools.partial(kernel, nz, ny), out_shape=jax.ShapeDtyp...  26.1 us
    unnamed x1, local copies, waits for them, and re-layouts  1.62 us

profile of v4, /device:TPU:0, one launch (start us, length us, event | category | flops | bytes accessed | tf_op | source)
XLA Modules:
  0.0 30.4 jit_solution(4471364535402278785)
XLA Ops:
  2.6 26.1 %shard_map.82 = f32[384,128]{1,0:T(8,128)} custom-call(bf16[384,2048]{1,0:T(8,128)(2,1)} %integ_hbm.1, bf16[384,128]{1,0:T(8,128)(2,1)} %probes_hbm.1, f32[250,128]{1,0:T(8,128)} %bitcast.1, f32[8000]{0:T(1024)} %occ_hbm.1, s32[1]{0:T(128)S(6)} %copy.10.bocc_hbm, s32[1]{0:T(128)S(6)} %copy.11.bvir_hbm, s32[1]{0:T(128)S(6)} %copy.12.bcount_hbm, ...), custom_call_target="tpu_custom_call" | custom-call | flops 402653184 | bytes 1572864 | tf_op jit(solution)/shard_map/pallas_call | solution.py:235
  28.7 1.6 %copy.14 = f32[384,128]{1,0:T(8,128)} copy(f32[384,128]{1,0:T(8,128)} %shard_map.82) | data formatting | bytes 393216

commit v5 on v4

--- a/solution.py
+++ b/solution.py
@@ -174,9 +174,9 @@
             per = rows_a // rows_r
             gathered[me, h // per, (h % per) * rows_r:(h % per + 1) * rows_r] = value
         while (done + 1) * rows_a <= (h + 1) * rows_r:
-            to_z(done)
             if ny > 1:
                 to_y(z, done)
+            to_z(done)
             spread(z, y, done)
             done += 1
     arrivals = [z] + [lax.rem(z + nz - d, nz) for d in ag_steps]

time: 30.6 us -> 30.6 us (level)
  no operation moved by 1% of the time
where the time goes in v5:
time: 30.6 us; the launch traced here: 30.3 us
  Pallas kernels  26.1 us (85%)
  between operations  2.59 us (8%)
  local copies, waits for them, and re-layouts  1.62 us (5%)
    pallas_call x1, Pallas kernels, on_device(): pl.pallas_call(functools.partial(kernel, nz, ny), out_shape=jax.ShapeDtyp...  26.1 us
    unnamed x1, local copies, waits for them, and re-layouts  1.62 us

profile of v5, /device:TPU:0, one launch (start us, length us, event | category | flops | bytes accessed | tf_op | source)
XLA Modules:
  0.0 30.3 jit_solution(12392750765919004543)
XLA Ops:
  2.6 26.1 %shard_map.82 = f32[384,128]{1,0:T(8,128)} custom-call(bf16[384,2048]{1,0:T(8,128)(2,1)} %integ_hbm.1, bf16[384,128]{1,0:T(8,128)(2,1)} %probes_hbm.1, f32[250,128]{1,0:T(8,128)} %bitcast.1, f32[8000]{0:T(1024)} %occ_hbm.1, s32[1]{0:T(128)S(6)} %copy.10.bocc_hbm, s32[1]{0:T(128)S(6)} %copy.11.bvir_hbm, s32[1]{0:T(128)S(6)} %copy.12.bcount_hbm, ...), custom_call_target="tpu_custom_call" | custom-call | flops 402653184 | bytes 1572864 | tf_op jit(solution)/shard_map/pallas_call | solution.py:235
  28.7 1.6 %copy.14 = f32[384,128]{1,0:T(8,128)} copy(f32[384,128]{1,0:T(8,128)} %shard_map.82) | data formatting | bytes 393216
